TPU v7x, 32 devices: a whole 2x2x4 slice. The times are simulated.
32 devices in a mesh: section: 2 (over core), head: 4 (over z), blk: 4 (over y, x).
Axes of the slice: x: 2, y: 2, z: 4, core: 2. Of those that a mesh axis runs over, the one named last changes fastest.
Arguments:
- section_input: bfloat16 [2, 8, 256, 1536], P('section', 'blk')
- modulation: bfloat16 [2, 8, 2, 1536], P('section', 'blk'), may hold values from -3 to 3
- attn_gate: bfloat16 [2, 8, 1536], P('section', 'blk'), may hold values from -12 to 12
- qkv_weight: bfloat16 [2, 1536, 3, 1536], P('section', None, None, 'head'), may hold values from -0.15625 to 0.15625
- out_weight: bfloat16 [2, 1536, 1536], P('section', 'head'), may hold values from -0.15625 to 0.15625
- kv_cache: bfloat16 [2, 8, 256, 4, 2, 1536], P('section', None, 'blk', None, None, 'head'), may hold values from -9 to 9
- text_kv: bfloat16 [2, 8, 154, 2, 1536], P('section', 'blk', None, None, 'head')
- text_len: int32 [8], P('blk'), may hold values from 4 to 154, as said below
- patch_order: int32 [4, 4], replicated, may hold values from 0 to 3, each once within a row
- final_mod: bfloat16 [8, 2, 1536], P('blk'), may hold values from -3 to 3
- final_weight: bfloat16 [1536, 64], replicated, may hold values from -0.15625 to 0.15625
- latent: float32 [4, 128, 128], P('blk', 'section'), may hold values from -6 to 6
Outputs:
- section_output: bfloat16 [2, 8, 256, 1536], P('section', 'blk', None, 'head')
- cache_patch: bfloat16 [2, 8, 256, 2, 1536], P('section', None, 'blk', None, 'head')
- latent_next: float32 [4, 128, 128], P('blk', 'section')
Inputs may be any that keep to these rules, and one draw needn't show every extreme that they name: `text_len`: sequence 0 uses all 154 text positions. `patch_order`: each row is a permutation of the 4 patches.
All inputs are finite; a program needn't handle non-finite values.
Results may differ from a plain program's by a relative error of at most 0.0092.
Values may be sent and summed in bfloat16 or wider, within the bound.
A program may use at most 128 MiB of HBM per device.

v0:
```python
import jax
import jax.numpy as jnp
from jax import lax
from jax.sharding import PartitionSpec as P

HEAD_DIM = 64
norm_eps = 1e-06
guidance = 4.0
euler_step = -0.25


def passed_along(shard, axis, by):
    devices = lax.axis_size(axis)
    return lax.ppermute(shard, axis, [(i, (i + by) % devices) for i in range(devices)])


def layer_norm(values):
    row_mean = jnp.mean(values, axis=-1, keepdims=True)
    centered = values - row_mean
    row_var = jnp.mean(centered * centered, axis=-1, keepdims=True)
    return centered / jnp.sqrt(row_var + norm_eps)


def piece_scores(query_heads, key_piece, counted_piece):
    seq_dev = key_piece.shape[0]
    head_count = query_heads.shape[2]
    key_heads = key_piece.reshape(seq_dev, -1, head_count, HEAD_DIM)
    scores = jnp.einsum(
        "sqhd,skhd->shqk", query_heads, key_heads, preferred_element_type=jnp.float32
    ) * HEAD_DIM ** (-0.5)
    if counted_piece is not None:
        scores = jnp.where(counted_piece[:, None, None, :], scores, -1e30)
    return scores


def piece_values(probs_piece, value_piece, head_count):
    seq_dev = value_piece.shape[0]
    value_heads = value_piece.reshape(seq_dev, -1, head_count, HEAD_DIM)
    return jnp.einsum(
        "shqk,skhd->sqhd", probs_piece, value_heads, preferred_element_type=jnp.float32
    )


def shards(
    section_input,
    modulation,
    attn_gate,
    qkv_weight,
    out_weight,
    kv_cache,
    text_kv,
    text_len,
    patch_order,
    final_mod,
    final_weight,
    latent,
):
    section_index = lax.axis_index("section")
    seq_patch = jnp.repeat(
        lax.dynamic_index_in_dim(patch_order, section_index, 1, keepdims=False), 2
    )
    hidden_in = section_input[0]
    seq_dev, patch_rows, model_width = hidden_in.shape
    own_patch = lax.dynamic_slice_in_dim(seq_patch, lax.axis_index("blk") * seq_dev, seq_dev, 0)
    hidden_wide = hidden_in.astype(jnp.float32)
    shift_scale = modulation[0].astype(jnp.float32)
    normed = (layer_norm(hidden_wide) * (1.0 + shift_scale[:, 1:2]) + shift_scale[:, 0:1]).astype(
        jnp.bfloat16
    )
    group_width = qkv_weight.shape[3]
    projected = jnp.dot(
        normed.reshape(seq_dev * patch_rows, model_width),
        qkv_weight[0].reshape(model_width, 3 * group_width),
        preferred_element_type=jnp.float32,
    ).astype(jnp.bfloat16)
    projected = projected.reshape(seq_dev, patch_rows, 3, group_width)
    queries = projected[:, :, 0]
    key_new = projected[:, :, 1]
    value_new = projected[:, :, 2]
    fresh_kv = jnp.stack([key_new, value_new], axis=2)
    refreshed = lax.all_to_all(fresh_kv, "blk", split_axis=1, concat_axis=0, tiled=True)
    local_cache = kv_cache[0]
    patch_count = local_cache.shape[2]
    fetched = lax.all_to_all(local_cache, "blk", split_axis=0, concat_axis=1, tiled=True)
    keep_patch = jnp.arange(patch_count, dtype=jnp.int32)[None, :] != own_patch[:, None]
    stale_counted = jnp.tile(keep_patch, (1, patch_rows))
    stale_keys = fetched[:, :, :, 0].reshape(seq_dev, -1, group_width)
    stale_values = fetched[:, :, :, 1].reshape(seq_dev, -1, group_width)
    text_local = text_kv[0]
    text_count = text_local.shape[1]
    text_counted = jnp.arange(text_count, dtype=jnp.int32)[None, :] < text_len[:, None]
    head_count = group_width // HEAD_DIM
    query_heads = queries.reshape(seq_dev, patch_rows, head_count, HEAD_DIM)
    text_scores = piece_scores(query_heads, text_local[:, :, 0], text_counted)
    fresh_scores = piece_scores(query_heads, key_new, None)
    stale_scores = piece_scores(query_heads, stale_keys, stale_counted)
    row_max = jnp.maximum(
        jnp.maximum(
            jnp.max(text_scores, axis=-1, keepdims=True),
            jnp.max(fresh_scores, axis=-1, keepdims=True),
        ),
        jnp.max(stale_scores, axis=-1, keepdims=True),
    )
    text_weights = jnp.exp(text_scores - row_max)
    fresh_weights = jnp.exp(fresh_scores - row_max)
    stale_weights = jnp.exp(stale_scores - row_max)
    total = (
        jnp.sum(text_weights, axis=-1, keepdims=True)
        + jnp.sum(fresh_weights, axis=-1, keepdims=True)
        + jnp.sum(stale_weights, axis=-1, keepdims=True)
    )
    text_probs = (text_weights / total).astype(jnp.bfloat16)
    fresh_probs = (fresh_weights / total).astype(jnp.bfloat16)
    stale_probs = (stale_weights / total).astype(jnp.bfloat16)
    attended_wide = (
        piece_values(text_probs, text_local[:, :, 1], head_count)
        + piece_values(fresh_probs, value_new, head_count)
        + piece_values(stale_probs, stale_values, head_count)
    )
    attended = attended_wide.astype(jnp.bfloat16)
    partial_value = jnp.dot(
        attended.reshape(seq_dev * patch_rows, group_width),
        out_weight[0],
        preferred_element_type=jnp.float32,
    )
    gate_wide = attn_gate[0].astype(jnp.float32)[:, None, :]
    share_width = model_width // lax.axis_size("head")
    share_start = lax.axis_index("head") * share_width
    half_rows = patch_rows // 2
    share_sum = lax.psum_scatter(
        partial_value.reshape(seq_dev, patch_rows, model_width).astype(jnp.bfloat16),
        "head",
        scatter_dimension=2,
        tiled=True,
    ).astype(jnp.float32)
    own_hidden = lax.dynamic_slice_in_dim(hidden_wide, share_start, share_width, 2)
    own_gate = lax.dynamic_slice_in_dim(gate_wide, share_start, share_width, 2)
    layer_out = (own_hidden + own_gate * share_sum).astype(jnp.bfloat16)
    received = passed_along(layer_out, "section", 1)
    last_layer = jnp.where(section_index == 0, received, layer_out)
    last_half = lax.dynamic_slice_in_dim(last_layer, section_index * half_rows, half_rows, 1)
    final_rows = lax.all_gather(last_half, "head", axis=2, tiled=True)
    final_shift = final_mod.astype(jnp.float32)
    final_normed = (
        layer_norm(final_rows.astype(jnp.float32)) * (1.0 + final_shift[:, 1:2])
        + final_shift[:, 0:1]
    ).astype(jnp.bfloat16)
    velocity = jnp.dot(
        final_normed.reshape(seq_dev * half_rows, model_width),
        final_weight,
        preferred_element_type=jnp.float32,
    )
    velocity = velocity.reshape(seq_dev // 2, 2, -1)
    guided = velocity[:, 1] + guidance * (velocity[:, 0] - velocity[:, 1])
    latent_next = latent + euler_step * guided.reshape(latent.shape)
    return (received[None], refreshed[None], latent_next)


def solution(mesh):
    placed = (
        P("section", "blk", None, None),
        P("section", "blk", None, None),
        P("section", "blk", None),
        P("section", None, None, "head"),
        P("section", "head", None),
        P("section", None, "blk", None, None, "head"),
        P("section", "blk", None, None, "head"),
        P("blk"),
        P(),
        P("blk", None, None),
        P(),
        P("blk", "section", None),
    )
    return jax.shard_map(
        shards,
        mesh=mesh,
        in_specs=placed,
        out_specs=(
            P("section", "blk", None, "head"),
            P("section", None, "blk", None, "head"),
            P("blk", "section", None),
        ),
        check_vma=False,
    )
```

profile of v0, /device:TPU:0, one launch (start us, length us, event | category | flops | bytes accessed | tf_op | source)
XLA Modules:
  0.0 174.6 jit_solution(1458555649823151610)
XLA Ops:
  7.2 5.4 %all-to-all-start = ((bf16[8,64,4,2,384]{4,3,2,1,0:T(2,128)(2,1)}), bf16[8,64,4,2,384]{4,3,2,1,0:T(2,128)(2,1)}, u32[]{:S(2)}, u32[]{:S(2)}) async-start(bf16[8,64,4,2,384]{4,3,2,1,0:T(2,128)(2,1)} %bitcast.90), calls=%async_computation | async-start | bytes 6291456 | tf_op jit(solution)/shard_map/all_to_all | solution.py:84
  14.3 6.1 %copy.85 = bf16[1,1536,3,384]{1,3,2,0:T(8,128)(2,1)} copy(bf16[1,1536,3,384]{3,1,2,0:T(8,128)(2,1)} %param.15) | data formatting | bytes 7077888 | tf_op args[3]
  21.1 5.2 %convolution_convert_fusion = bf16[512,1152]{1,0:T(8,128)(2,1)} fusion(bf16[512,1536]{1,0:T(8,128)(2,1)S(1)} %bitcast.95, bf16[1536,1152]{0,1:T(8,128)(2,1)} %bitcast.89), kind=kOutput, calls=%fused_computation.14 | convolution fusion | flops 1812529152 | bytes 6291456 | tf_op jit(solution)/shard_map/dot_general | solution.py:71
  26.3 2.4 %copy.86 = bf16[512,1152]{0,1:T(8,128)(2,1)} copy(bf16[512,1152]{1,0:T(8,128)(2,1)} %convolution_convert_fusion) | data formatting | bytes 2359296 | tf_op jit(solution)/shard_map/convert_element_type | solution.py:75
  28.7 3.7 %reshape.237 = bf16[2,256,3,384]{1,0,3,2:T(2,128)(2,1)} reshape(bf16[512,1152]{0,1:T(8,128)(2,1)} %copy.86) | data formatting | bytes 2359296 | tf_op jit(solution)/shard_map/reshape | solution.py:76
  32.4 2.1 %fusion.35 = (bf16[2,256,1,384]{1,0,3,2:T(2,128)(2,1)S(1)}, bf16[2,256,1,384]{1,0,3,2:T(2,128)(2,1)S(1)}, bf16[2,256,1,384]{1,0,3,2:T(2,128)(2,1)S(1)}) fusion(bf16[2,256,3,384]{1,0,3,2:T(2,128)(2,1)} %reshape.237), kind=kLoop, calls=%fused_computation.71 | loop fusion | bytes 2359296 | tf_op jit(solution)/shard_map/slice | solution.py:79
  37.0 2.0 %copy.88 = bf16[2,154,1,384]{1,3,0,2:T(8,128)(2,1)} copy(bf16[2,154,1,384]{3,2,1,0:T(2,128)(2,1)} %get-tuple-element.18) | data formatting | bytes 473088 | tf_op jit(solution)/shard_map/slice | solution.py:94
  39.7 2.0 %copy.92 = bf16[2,154,1,384]{1,3,0,2:T(8,128)(2,1)} copy(bf16[2,154,1,384]{3,2,1,0:T(2,128)(2,1)} %get-tuple-element.17) | data formatting | bytes 473088 | tf_op jit(solution)/shard_map/slice | solution.py:116
  41.9 3.5 %fusion.9 = (f32[2,6,256]{2,1,0:T(8,128)}, f32[2,6,256,154]{2,3,1,0:T(8,128)}) fusion(pred[2,154]{1,0:T(4,128)(4,1)S(1)} %iota_compare_fusion, bf16[2,256,6,64]{1,3,2,0:T(8,128)(2,1)S(1)} %bitcast.86, bf16[2,154,6,64]{1,3,2,0:T(8,128)(2,1)} %bitcast.96), kind=kOutput, calls=%fused_computation.26 | convolution fusion | flops 61971456 | bytes 2534708 | tf_op jit(solution)/shard_map/sqhd,skhd->shqk/dot_general | solution.py:28
  45.3 2.9 %multiply_reduce_fusion.1 = (f32[2,6,256]{2,1,0:T(8,128)}, f32[2,6,256,256]{2,3,1,0:T(8,128)}) fusion(bf16[2,256,6,64]{1,3,2,0:T(8,128)(2,1)S(1)} %bitcast.87, bf16[2,256,6,64]{1,3,2,0:T(8,128)(2,1)S(1)} %bitcast.98), kind=kOutput, calls=%fused_computation.16 | convolution fusion | flops 102233088 | bytes 3944448 | tf_op jit(solution)/shard_map/sqhd,skhd->shqk/dot_general | solution.py:28
  48.2 1.6 all-to-all-done
  49.8 3.4 %copy.90 = bf16[2,4,64,4,2,384]{5,3,2,1,0,4:T(4,128)(2,1)S(1)} copy(bf16[2,4,64,4,2,384]{5,4,3,2,0,1:T(2,128)(2,1)} %bitcast.13) | data formatting | bytes 6291456 | tf_op jit(solution)/shard_map/all_to_all | solution.py:84
  53.2 2.8 %fusion.34 = (bf16[2,256,4,1,384]{4,2,1,0,3:T(4,128)(2,1)}, bf16[2,256,4,1,384]{4,2,1,0,3:T(4,128)(2,1)}) fusion(bf16[2,256,4,2,384]{4,2,1,0,3:T(4,128)(2,1)S(1)} %bitcast.83), kind=kLoop, calls=%fused_computation.70 | loop fusion | bytes 6291456 | tf_op jit(solution)/shard_map/slice | solution.py:87
  56.0 6.0 %reshape_reshape_squeeze.6 = bf16[2,1024,6,64]{3,2,1,0:T(8,128)(2,1)} reshape(bf16[2,256,4,1,384]{4,2,1,0,3:T(4,128)(2,1)} %get-tuple-element.12) | data formatting | bytes 3145728 | tf_op jit(solution)/shard_map/reshape;reshape;squeeze | solution.py:27
  62.0 4.4 %fusion = (f32[2,6,256]{2,1,0:T(8,128)S(1)}, f32[2,6,256,1024]{3,2,1,0:T(8,128)S(1)}) fusion(pred[2,1024]{1,0:T(4,128)(4,1)S(1)} %tile.9, bf16[2,256,6,64]{1,3,2,0:T(8,128)(2,1)S(1)} %bitcast.88, bf16[2,1024,6,64]{3,2,1,0:T(8,128)(2,1)} %reshape_reshape_squeeze.6), kind=kOutput, calls=%fused_computation.3 | convolution fusion | flops 412087296 | bytes 14563328 | tf_op jit(solution)/shard_map/sqhd,skhd->shqk/dot_general | solution.py:28
  66.5 3.3 %fusion.1 = f32[2,6,256]{2,1,0:T(8,128)S(1)} fusion(f32[2,6,256,1024]{3,2,1,0:T(8,128)S(1)} %get-tuple-element.24, f32[2,6,256]{2,1,0:T(8,128)S(1)} %maximum_maximum_fusion, pred[2,1024]{1,0:T(4,128)(4,1)S(1)} %tile.9), kind=kLoop, calls=%fused_computation.4 | loop fusion | flops 12579840 | bytes 12609536 | tf_op jit(solution)/shard_map/reduce_sum | solution.py:110
  69.8 2.0 %copy-done.1 = f32[2,6,256,1024]{3,2,1,0:T(8,128)} copy-done((f32[2,6,256,1024]{3,2,1,0:T(8,128)}, f32[2,6,256,1024]{3,2,1,0:T(8,128)S(1)}, u32[]{:S(2)}) %copy-start.1) | copy-done | bytes 12582936
  73.9 6.1 %reshape_reshape_squeeze.7 = bf16[2,1024,6,64]{3,2,1,0:T(8,128)(2,1)} reshape(bf16[2,256,4,1,384]{4,2,1,0,3:T(4,128)(2,1)} %get-tuple-element.13) | data formatting | bytes 3145728 | tf_op jit(solution)/shard_map/reshape;reshape;squeeze | solution.py:38
  80.0 2.8 %fusion.16 = f32[2,256,6,64]{1,3,2,0:T(8,128)S(1)} fusion(bf16[2,256,6,64]{1,3,2,0:T(8,128)(2,1)S(1)} %bitcast.101, f32[2,6,256,256]{2,3,1,0:T(8,128)} %get-tuple-element.28, f32[2,6,256]{2,1,0:T(8,128)S(1)} %add_add_fusion, f32[2,6,256]{2,1,0:T(8,128)S(1)} %maximum_maximum_fusion), kind=kOutput, calls=%fused_computation.33 | convolution fusion | flops 103809024 | bytes 4349952 | tf_op jit(solution)/shard_map/shqk,skhd->sqhd/dot_general | solution.py:39
  82.8 2.7 %copy-done.2 = f32[2,6,256,1024]{3,2,1,0:T(8,128)S(1)} copy-done((f32[2,6,256,1024]{3,2,1,0:T(8,128)S(1)}, f32[2,6,256,1024]{3,2,1,0:T(8,128)}, u32[]{:S(2)}) %copy-start.2) | copy-done | bytes 12582936
  85.5 5.7 %fusion.19 = f32[2,256,6,64]{1,3,2,0:T(8,128)S(1)} fusion(bf16[2,1024,6,64]{3,2,1,0:T(8,128)(2,1)} %reshape_reshape_squeeze.7, f32[2,6,256,1024]{3,2,1,0:T(8,128)S(1)} %copy-done.2, f32[2,6,256]{2,1,0:T(8,128)S(1)} %add_add_fusion, f32[2,6,256]{2,1,0:T(8,128)S(1)} %maximum_maximum_fusion, pred[2,1024]{1,0:T(4,128)(4,1)S(1)} %tile.9), kind=kOutput, calls=%fused_computation.37 | convolution fusion | flops 418381824 | bytes 14968832 | tf_op jit(solution)/shard_map/shqk,skhd->sqhd/dot_general | solution.py:39
  91.9 2.2 %convolution_convert_fusion.1 = bf16[2,256,1536]{2,1,0:T(8,128)(2,1)} fusion(bf16[2,256,384]{1,2,0:T(8,128)(2,1)S(1)} %bitcast.99, bf16[1,384,1536]{2,1,0:T(8,128)(2,1)S(1)} %copy-done), kind=kOutput, calls=%fused_computation.15 | convolution fusion | flops 604766208 | bytes 3145728 | tf_op jit(solution)/shard_map/dot_general | solution.py:121
  94.1 4.9 %copy.105 = bf16[2,256,1536]{1,0,2:T(2,128)(2,1)} copy(bf16[2,256,1536]{2,1,0:T(8,128)(2,1)} %convolution_convert_fusion.1) | data formatting | bytes 3145728
  99.0 3.0 %copy.111 = bf16[192,8,2,256]{3,1,2,0:T(8,128)(2,1)} copy(bf16[192,8,2,256]{3,2,1,0:T(2,128)(2,1)} %bitcast.85) | data formatting | bytes 3145728
  102.0 2.9 %copy.97 = bf16[2,256,2,384]{3,2,0,1:T(2,128)(2,1)} copy(bf16[2,256,2,384]{1,0,3,2:T(2,128)(2,1)S(1)} %slice-done) | data formatting | bytes 1572864 | tf_op jit(solution)/shard_map/stack | solution.py:80
  104.9 3.6 %all-to-all-start.1 = ((bf16[2,256,2,384]{3,2,0,1:T(2,128)(2,1)}), bf16[2,256,2,384]{3,2,0,1:T(2,128)(2,1)S(1)}, u32[]{:S(2)}, u32[]{:S(2)}) async-start(bf16[2,256,2,384]{3,2,0,1:T(2,128)(2,1)} %copy.97), calls=%async_computation.1 | async-start | bytes 1572864 | tf_op jit(solution)/shard_map/all_to_all | solution.py:81
  108.5 2.1 %convert_element_type.70 = f32[1,2,256,1536]{3,2,1,0:T(8,128)} convert(bf16[1,2,256,1536]{3,2,1,0:T(8,128)(2,1)S(1)} %copy-done.3) | non-fusion elementwise | flops 786432 | bytes 4718592 | tf_op jit(solution)/shard_map/convert_element_type | solution.py:65
  111.3 27.1 %reduce-scatter.4.cloned.1.call-done = bf16[384,512]{1,0:T(8,128)(2,1)} async-done(((bf16[1536,512]{1,0:T(8,128)(2,1)}), bf16[384,512]{1,0:T(8,128)(2,1)}) %reduce-scatter.4.cloned.1.call-update) | async-done | bytes 393232
  140.2 2.0 %fusion.28 = bf16[2,256,384]{2,1,0:T(8,128)(2,1)} fusion(bf16[2,256,384]{2,1,0:T(8,128)(2,1)S(1)} %copy.106, f32[1,2,256,1536]{3,2,1,0:T(8,128)} %convert_element_type.70, s32[]{:T(128)S(6)} %select_n.30, f32[2,384]{1,0:T(2,128)S(1)} %convert_bitcast_fusion), kind=kLoop, calls=%fused_computation.45 | loop fusion | flops 786432 | bytes 1575940 | tf_op jit(solution)/shard_map/convert_element_type | solution.py:138
  143.0 1.7 copy.101
  145.8 18.0 %all_gather.3 = bf16[2,128,1536]{2,1,0:T(8,128)(2,1)S(1)} all-gather(bf16[2,128,384]{2,1,0:T(8,128)(2,1)S(1)} %dynamic-slice_select_fusion), channel_id=1, replica_groups=mesh['section'=2,'head'=4,'blk'=4] {'head'}, dimensions={2}, use_global_device_ids=true | all-gather | bytes 983040 | tf_op jit(solution)/shard_map/all_gather | solution.py:142
  165.9 1.8 %copy.125 = bf16[1,2,256,384]{3,2,1,0:T(8,128)(2,1)} copy(bf16[1,2,256,384]{3,2,1,0:T(8,128)(2,1)} %bitcast.23) | data formatting | bytes 786432
  (89 shorter events, 14.8 us)
Async XLA Ops:
  7.2 84.8 %copy-start = (bf16[1,384,1536]{2,1,0:T(8,128)(2,1)S(1)}, bf16[1,384,1536]{2,1,0:T(8,128)(2,1)}, u32[]{:S(2)}) copy-start(bf16[1,384,1536]{2,1,0:T(8,128)(2,1)} %param.16) | copy-start | bytes 3538948
  7.2 5.5 %copy-start.18 = (s32[4,4]{1,0:T(4,128)S(1)}, s32[4,4]{1,0:T(4,128)}, u32[]{:S(2)}) copy-start(s32[4,4]{1,0:T(4,128)} %param.20) | copy-start | bytes 196
  7.2 6.2 %copy-start.17 = (bf16[1,2,2,1536]{3,2,1,0:T(2,128)(2,1)S(1)}, bf16[1,2,2,1536]{3,2,1,0:T(2,128)(2,1)}, u32[]{:S(2)}) copy-start(bf16[1,2,2,1536]{3,2,1,0:T(2,128)(2,1)} %param.13) | copy-start | bytes 36868
  7.2 6.3 %copy-start.3 = (bf16[1,2,256,1536]{3,2,1,0:T(8,128)(2,1)S(1)}, bf16[1,2,256,1536]{3,2,1,0:T(8,128)(2,1)}, u32[]{:S(2)}) copy-start(bf16[1,2,256,1536]{3,2,1,0:T(8,128)(2,1)} %param.12) | copy-start | bytes 4718596
  7.2 42.6 %all-to-all-start = ((bf16[8,64,4,2,384]{4,3,2,1,0:T(2,128)(2,1)}), bf16[8,64,4,2,384]{4,3,2,1,0:T(2,128)(2,1)}, u32[]{:S(2)}, u32[]{:S(2)}) async-start(bf16[8,64,4,2,384]{4,3,2,1,0:T(2,128)(2,1)} %bitcast.90), calls=%async_computation | async-start | bytes 6291456 | tf_op jit(solution)/shard_map/all_to_all | solution.py:84
  12.6 125.8 %reduce-scatter.4.cloned.1.call-start = ((), (), s32[]{:S(2)}) async-start(), calls=%async_computation.3 | async-start | bytes 1966080
  32.4 3.0 %copy-start.7 = (bf16[1,2,154,2,384]{4,3,2,1,0:T(2,128)(2,1)S(1)}, bf16[1,2,154,2,384]{4,3,2,1,0:T(2,128)(2,1)}, u32[]{:S(2)}) copy-start(bf16[1,2,154,2,384]{4,3,2,1,0:T(2,128)(2,1)} %param.18) | copy-start | bytes 1419268
  34.5 7.3 %copy-start.19 = (s32[2]{0:T(128)S(1)}, s32[2]{0:T(128)}, u32[]{:S(2)}) copy-start(s32[2]{0:T(128)} %param.19) | copy-start | bytes 28
  39.7 5.6 %copy-start.8 = (bf16[2,256,1,384]{1,3,0,2:T(8,128)(2,1)S(1)}, bf16[2,256,1,384]{1,3,0,2:T(8,128)(2,1)}, u32[]{:S(2)}) copy-start(bf16[2,256,1,384]{1,3,0,2:T(8,128)(2,1)} %copy.89) | copy-start | bytes 1179652
  62.0 4.5 %copy-start.12 = (f32[2,6,256]{2,1,0:T(8,128)S(1)}, f32[2,6,256]{2,1,0:T(8,128)}, u32[]{:S(2)}) copy-start(f32[2,6,256]{2,1,0:T(8,128)} %get-tuple-element.25) | copy-start | bytes 36868
  62.0 4.5 %copy-start.13 = (f32[2,6,256]{2,1,0:T(8,128)S(1)}, f32[2,6,256]{2,1,0:T(8,128)}, u32[]{:S(2)}) copy-start(f32[2,6,256]{2,1,0:T(8,128)} %get-tuple-element.27) | copy-start | bytes 36868
  66.5 5.3 %copy-start.1 = (f32[2,6,256,1024]{3,2,1,0:T(8,128)}, f32[2,6,256,1024]{3,2,1,0:T(8,128)S(1)}, u32[]{:S(2)}) copy-start(f32[2,6,256,1024]{3,2,1,0:T(8,128)S(1)} %get-tuple-element.24) | copy-start | bytes 37748740
  66.5 5.3 %copy-start.4 = (f32[2,6,256,256]{2,3,1,0:T(8,128)S(1)}, f32[2,6,256,256]{2,3,1,0:T(8,128)}, u32[]{:S(2)}) copy-start(f32[2,6,256,256]{2,3,1,0:T(8,128)} %get-tuple-element.28) | copy-start | bytes 9437188
  71.8 1.5 copy-start.5
  73.8 6.2 %copy-start.10 = (bf16[2,256,1,384]{1,3,0,2:T(8,128)(2,1)S(1)}, bf16[2,256,1,384]{1,3,0,2:T(8,128)(2,1)}, u32[]{:S(2)}) copy-start(bf16[2,256,1,384]{1,3,0,2:T(8,128)(2,1)} %copy.93) | copy-start | bytes 1179652
  80.0 5.5 %copy-start.2 = (f32[2,6,256,1024]{3,2,1,0:T(8,128)S(1)}, f32[2,6,256,1024]{3,2,1,0:T(8,128)}, u32[]{:S(2)}) copy-start(f32[2,6,256,1024]{3,2,1,0:T(8,128)} %copy-done.1) | copy-start | bytes 37748740
  85.5 5.7 %copy-start.6 = (f32[2,6,256,154]{2,3,1,0:T(8,128)S(1)}, f32[2,6,256,154]{2,3,1,0:T(8,128)}, u32[]{:S(2)}) copy-start(f32[2,6,256,154]{2,3,1,0:T(8,128)} %get-tuple-element.26) | copy-start | bytes 5677060
  85.5 5.7 %copy-start.9 = (bf16[2,154,1,384]{1,3,0,2:T(8,128)(2,1)S(1)}, bf16[2,154,1,384]{1,3,0,2:T(8,128)(2,1)}, u32[]{:S(2)}) copy-start(bf16[2,154,1,384]{1,3,0,2:T(8,128)(2,1)} %copy.92) | copy-start | bytes 709636
  99.0 3.0 %slice-start = ((bf16[2,256,3,384]{1,0,3,2:T(2,128)(2,1)}), bf16[2,256,2,384]{1,0,3,2:T(2,128)(2,1)S(1)}, s32[]{:S(2)}) async-start(bf16[2,256,3,384]{1,0,3,2:T(2,128)(2,1)} %reshape.237), calls=%async_computation.4 | async-start | bytes 1572864 | tf_op jit(solution)/shard_map/stack | solution.py:80
  104.9 5.7 %copy-start.15 = (bf16[2,2,1536]{2,1,0:T(2,128)(2,1)S(1)}, bf16[2,2,1536]{2,1,0:T(2,128)(2,1)}, u32[]{:S(2)}) copy-start(bf16[2,2,1536]{2,1,0:T(2,128)(2,1)} %param.21) | copy-start | bytes 36868
  104.9 37.9 %all-to-all-start.1 = ((bf16[2,256,2,384]{3,2,0,1:T(2,128)(2,1)}), bf16[2,256,2,384]{3,2,0,1:T(2,128)(2,1)S(1)}, u32[]{:S(2)}, u32[]{:S(2)}) async-start(bf16[2,256,2,384]{3,2,0,1:T(2,128)(2,1)} %copy.97), calls=%async_computation.1 | async-start | bytes 1572864 | tf_op jit(solution)/shard_map/all_to_all | solution.py:81
  142.2 2.5 %collective-permute-start = (bf16[2,256,384]{2,1,0:T(8,128)(2,1)}, bf16[2,256,384]{2,1,0:T(8,128)(2,1)}, u32[]{:S(2)}, u32[]{:S(2)}) collective-permute-start(bf16[2,256,384]{2,1,0:T(8,128)(2,1)} %fusion.28), channel_id=1, source_target_pairs={{0,16},{16,0},{1,17},{17,1},{2,18},{18,2},{3,19},{19,3},{4,20},{20... | collective-permute-start | bytes 1179656 | tf_op jit(solution)/shard_map/ppermute | solution.py:14
  142.9 21.5 %copy-start.14 = (f32[2,1536]{1,0:T(2,128)S(1)}, f32[2,1536]{1,0:T(2,128)}, u32[]{:S(2)}) copy-start(f32[2,1536]{1,0:T(2,128)} %get-tuple-element.32) | copy-start | bytes 36868
  143.0 21.7 %copy-start.11 = (bf16[1536,64]{0,1:T(8,128)(2,1)S(1)}, bf16[1536,64]{0,1:T(8,128)(2,1)}, u32[]{:S(2)}) copy-start(bf16[1536,64]{0,1:T(8,128)(2,1)} %param.22) | copy-start | bytes 589828
  144.7 20.6 %copy-start.16 = (f32[1,64,128]{2,1,0:T(8,128)S(1)}, f32[1,64,128]{2,1,0:T(8,128)}, u32[]{:S(2)}) copy-start(f32[1,64,128]{2,1,0:T(8,128)} %param.23) | copy-start | bytes 98308
Sparse Core Ops, SparseCore 0:
  102.1 36.2 reduce-scatter.3
where the time goes:
time: 176 us; the launch traced here: 175 us
  local copies, waits for them, and re-layouts  63.3 us (36%)
  waiting for transfers between devices  28.7 us (16%)
  matrix products  27.7 us (16%)
  blocking collectives  18 us (10%)
  between operations  14.4 us (8%)
  other arithmetic  13.4 us (8%)
  starting transfers between devices  9.07 us (5%)
    unnamed x2, waiting for transfers between devices  27.1 us
    unnamed x49, local copies, waits for them, and re-layouts  25.6 us
    all_gather x1, blocking collectives, shards(): final_rows = lax.all_gather(last_half, 'head', axis=2, tiled=True)  18 us
    dot_general x3, matrix products, piece_scores(): jnp.einsum('sqhd,skhd->shqk', query_heads, key_heads, preferred_element_t...  10.8 us
    dot_general x3, matrix products, piece_values(): jnp.einsum('shqk,skhd->sqhd', probs_piece, value_heads, preferred_element...  9.17 us
    another operation x1, local copies, waits for them, and re-layouts, piece_values(): value_heads = value_piece.reshape(seq_dev, -1, head_count, HEAD_DIM)  6.13 us
    another operation x1, local copies, waits for them, and re-layouts, piece_scores(): key_heads = key_piece.reshape(seq_dev, -1, head_count, HEAD_DIM)  6.03 us
    all_to_all x1, starting transfers between devices, shards(): lax.all_to_all(local_cache, 'blk', split_axis=0, concat_axis=1, tiled=True)  5.44 us
  transfers between devices with their start and end apart: 4, of which 2 were waited for; matrix products, arithmetic and copies ran while one was open for 27% of the time, Pallas kernels for 0%

commit v1 on v0

--- a/solution.py
+++ b/solution.py
@@ -139,7 +139,14 @@
     received = passed_along(layer_out, "section", 1)
     last_layer = jnp.where(section_index == 0, received, layer_out)
     last_half = lax.dynamic_slice_in_dim(last_layer, section_index * half_rows, half_rows, 1)
-    final_rows = lax.all_gather(last_half, "head", axis=2, tiled=True)
+    ways, here = (lax.axis_size("head"), lax.axis_index("head"))
+    final_rows, reach = (last_half, 1)
+    while reach < ways:
+        theirs = lax.ppermute(final_rows, "head", [(d, d ^ reach) for d in range(ways)])
+        mine_first = jnp.concatenate([final_rows, theirs], axis=2)
+        theirs_first = jnp.concatenate([theirs, final_rows], axis=2)
+        final_rows = jnp.where(here & reach == 0, mine_first, theirs_first)
+        reach = 2 * reach
     final_shift = final_mod.astype(jnp.float32)
     final_normed = (
         layer_norm(final_rows.astype(jnp.float32)) * (1.0 + final_shift[:, 1:2])

time: 176 us -> 188 us (1.068)
  waiting for transfers between devices: 28.7 us -> 55.9 us
  blocking collectives: 18 us -> 0 us
  starting transfers between devices: 9.07 us -> 11 us
    ppermute x0 -> x2, waiting for transfers between devices: none -> 20.1 us  [shards(): lax.ppermute(final_rows, 'head', [(d, d ^ reach) for d in range(ways)])]
    all_gather x1 -> x0, blocking collectives: 18 us -> none  [shards(): final_rows = lax.all_gather(last_half, 'head', axis=2, tiled=True)]
    unnamed x2, waiting for transfers between devices: 27.1 us -> 33.8 us
    ppermute x0 -> x2, starting transfers between devices: none -> 1.92 us  [shards(): lax.ppermute(final_rows, 'head', [(d, d ^ reach) for d in range(ways)])]
  transfers between devices with their start and end apart: 4 -> 6, of which waited for: 2 -> 5; matrix products, arithmetic and copies ran while one was open for 27% -> 25% of each run, Pallas kernels for 0% -> 0%
where the time goes in v1:
time: 188 us; the launch traced here: 187 us
  local copies, waits for them, and re-layouts  63.5 us (34%)
  waiting for transfers between devices  55.9 us (30%)
  matrix products  27.7 us (15%)
  between operations  14.4 us (8%)
  other arithmetic  14.1 us (8%)
  starting transfers between devices  11 us (6%)
    unnamed x2, waiting for transfers between devices  33.8 us
    unnamed x49, local copies, waits for them, and re-layouts  25.2 us
    ppermute x2, waiting for transfers between devices, shards(): lax.ppermute(final_rows, 'head', [(d, d ^ reach) for d in range(ways)])  20.1 us
    dot_general x3, matrix products, piece_scores(): jnp.einsum('sqhd,skhd->shqk', query_heads, key_heads, preferred_element_t...  10.8 us
    dot_general x3, matrix products, piece_values(): jnp.einsum('shqk,skhd->sqhd', probs_piece, value_heads, preferred_element...  9.17 us
    another operation x1, local copies, waits for them, and re-layouts, piece_values(): value_heads = value_piece.reshape(seq_dev, -1, head_count, HEAD_DIM)  6.16 us
    another operation x1, local copies, waits for them, and re-layouts, piece_scores(): key_heads = key_piece.reshape(seq_dev, -1, head_count, HEAD_DIM)  6.02 us
    all_to_all x1, starting transfers between devices, shards(): lax.all_to_all(local_cache, 'blk', split_axis=0, concat_axis=1, tiled=True)  5.44 us
  transfers between devices with their start and end apart: 6, of which 5 were waited for; matrix products, arithmetic and copies ran while one was open for 25% of the time, Pallas kernels for 0%

profile of v1, /device:TPU:0, one launch (start us, length us, event | category | flops | bytes accessed | tf_op | source)
XLA Modules:
  0.0 186.7 jit_solution(8921055538020342067)
XLA Ops:
  7.2 5.4 %all-to-all-start = ((bf16[8,64,4,2,384]{4,3,2,1,0:T(2,128)(2,1)}), bf16[8,64,4,2,384]{4,3,2,1,0:T(2,128)(2,1)}, u32[]{:S(2)}, u32[]{:S(2)}) async-start(bf16[8,64,4,2,384]{4,3,2,1,0:T(2,128)(2,1)} %bitcast.105), calls=%async_computation | async-start | bytes 6291456 | tf_op jit(solution)/shard_map/all_to_all | solution.py:84
  14.3 6.1 %copy.85 = bf16[1,1536,3,384]{1,3,2,0:T(8,128)(2,1)} copy(bf16[1,1536,3,384]{3,1,2,0:T(8,128)(2,1)} %param.15) | data formatting | bytes 7077888 | tf_op args[3]
  21.1 5.2 %convolution_convert_fusion = bf16[512,1152]{1,0:T(8,128)(2,1)} fusion(bf16[512,1536]{1,0:T(8,128)(2,1)S(1)} %bitcast.110, bf16[1536,1152]{0,1:T(8,128)(2,1)} %bitcast.103), kind=kOutput, calls=%fused_computation.14 | convolution fusion | flops 1812529152 | bytes 6291456 | tf_op jit(solution)/shard_map/dot_general | solution.py:71
  26.3 2.4 %copy.86 = bf16[512,1152]{0,1:T(8,128)(2,1)} copy(bf16[512,1152]{1,0:T(8,128)(2,1)} %convolution_convert_fusion) | data formatting | bytes 2359296 | tf_op jit(solution)/shard_map/convert_element_type | solution.py:75
  28.7 3.7 %reshape.258 = bf16[2,256,3,384]{1,0,3,2:T(2,128)(2,1)} reshape(bf16[512,1152]{0,1:T(8,128)(2,1)} %copy.86) | data formatting | bytes 2359296 | tf_op jit(solution)/shard_map/reshape | solution.py:76
  32.4 2.1 %fusion.33 = (bf16[2,256,1,384]{1,0,3,2:T(2,128)(2,1)S(1)}, bf16[2,256,1,384]{1,0,3,2:T(2,128)(2,1)S(1)}, bf16[2,256,1,384]{1,0,3,2:T(2,128)(2,1)S(1)}) fusion(bf16[2,256,3,384]{1,0,3,2:T(2,128)(2,1)} %reshape.258), kind=kLoop, calls=%fused_computation.75 | loop fusion | bytes 2359296 | tf_op jit(solution)/shard_map/slice | solution.py:79
  36.9 2.0 %copy.88 = bf16[2,154,1,384]{1,3,0,2:T(8,128)(2,1)} copy(bf16[2,154,1,384]{3,2,1,0:T(2,128)(2,1)} %get-tuple-element.18) | data formatting | bytes 473088 | tf_op jit(solution)/shard_map/slice | solution.py:94
  39.7 2.0 %copy.92 = bf16[2,154,1,384]{1,3,0,2:T(8,128)(2,1)} copy(bf16[2,154,1,384]{3,2,1,0:T(2,128)(2,1)} %get-tuple-element.17) | data formatting | bytes 473088 | tf_op jit(solution)/shard_map/slice | solution.py:116
  41.9 3.5 %fusion.7 = (f32[2,6,256]{2,1,0:T(8,128)}, f32[2,6,256,154]{2,3,1,0:T(8,128)}) fusion(pred[2,154]{1,0:T(4,128)(4,1)S(1)} %iota_compare_fusion, bf16[2,256,6,64]{1,3,2,0:T(8,128)(2,1)S(1)} %bitcast.100, bf16[2,154,6,64]{1,3,2,0:T(8,128)(2,1)} %bitcast.111), kind=kOutput, calls=%fused_computation.24 | convolution fusion | flops 61971456 | bytes 2534708 | tf_op jit(solution)/shard_map/sqhd,skhd->shqk/dot_general | solution.py:28
  45.3 2.9 %multiply_reduce_fusion.1 = (f32[2,6,256]{2,1,0:T(8,128)}, f32[2,6,256,256]{2,3,1,0:T(8,128)}) fusion(bf16[2,256,6,64]{1,3,2,0:T(8,128)(2,1)S(1)} %bitcast.101, bf16[2,256,6,64]{1,3,2,0:T(8,128)(2,1)S(1)} %bitcast.113), kind=kOutput, calls=%fused_computation.16 | convolution fusion | flops 102233088 | bytes 3944448 | tf_op jit(solution)/shard_map/sqhd,skhd->shqk/dot_general | solution.py:28
  48.2 1.6 all-to-all-done
  49.8 3.4 %copy.90 = bf16[2,4,64,4,2,384]{5,3,2,1,0,4:T(4,128)(2,1)S(1)} copy(bf16[2,4,64,4,2,384]{5,4,3,2,0,1:T(2,128)(2,1)} %bitcast.13) | data formatting | bytes 6291456 | tf_op jit(solution)/shard_map/all_to_all | solution.py:84
  53.2 2.8 %fusion.32 = (bf16[2,256,4,1,384]{4,2,1,0,3:T(4,128)(2,1)}, bf16[2,256,4,1,384]{4,2,1,0,3:T(4,128)(2,1)}) fusion(bf16[2,256,4,2,384]{4,2,1,0,3:T(4,128)(2,1)S(1)} %bitcast.97), kind=kLoop, calls=%fused_computation.74 | loop fusion | bytes 6291456 | tf_op jit(solution)/shard_map/slice | solution.py:87
  56.0 6.0 %reshape_reshape_squeeze.6 = bf16[2,1024,6,64]{3,2,1,0:T(8,128)(2,1)} reshape(bf16[2,256,4,1,384]{4,2,1,0,3:T(4,128)(2,1)} %get-tuple-element.12) | data formatting | bytes 3145728 | tf_op jit(solution)/shard_map/reshape;reshape;squeeze | solution.py:27
  62.1 4.4 %fusion = (f32[2,6,256]{2,1,0:T(8,128)S(1)}, f32[2,6,256,1024]{3,2,1,0:T(8,128)S(1)}) fusion(pred[2,1024]{1,0:T(4,128)(4,1)S(1)} %tile.9, bf16[2,256,6,64]{1,3,2,0:T(8,128)(2,1)S(1)} %bitcast.102, bf16[2,1024,6,64]{3,2,1,0:T(8,128)(2,1)} %reshape_reshape_squeeze.6), kind=kOutput, calls=%fused_computation.3 | convolution fusion | flops 412087296 | bytes 14563328 | tf_op jit(solution)/shard_map/sqhd,skhd->shqk/dot_general | solution.py:28
  66.6 3.3 %fusion.1 = f32[2,6,256]{2,1,0:T(8,128)S(1)} fusion(f32[2,6,256,1024]{3,2,1,0:T(8,128)S(1)} %get-tuple-element.26, f32[2,6,256]{2,1,0:T(8,128)S(1)} %maximum_maximum_fusion, pred[2,1024]{1,0:T(4,128)(4,1)S(1)} %tile.9), kind=kLoop, calls=%fused_computation.4 | loop fusion | flops 12579840 | bytes 12609536 | tf_op jit(solution)/shard_map/reduce_sum | solution.py:110
  69.8 2.0 %copy-done.1 = f32[2,6,256,1024]{3,2,1,0:T(8,128)} copy-done((f32[2,6,256,1024]{3,2,1,0:T(8,128)}, f32[2,6,256,1024]{3,2,1,0:T(8,128)S(1)}, u32[]{:S(2)}) %copy-start.1) | copy-done | bytes 12582936
  73.9 6.2 %reshape_reshape_squeeze.7 = bf16[2,1024,6,64]{3,2,1,0:T(8,128)(2,1)} reshape(bf16[2,256,4,1,384]{4,2,1,0,3:T(4,128)(2,1)} %get-tuple-element.13) | data formatting | bytes 3145728 | tf_op jit(solution)/shard_map/reshape;reshape;squeeze | solution.py:38
  80.0 2.8 %fusion.13 = f32[2,256,6,64]{1,3,2,0:T(8,128)S(1)} fusion(bf16[2,256,6,64]{1,3,2,0:T(8,128)(2,1)S(1)} %bitcast.118, f32[2,6,256,256]{2,3,1,0:T(8,128)} %get-tuple-element.30, f32[2,6,256]{2,1,0:T(8,128)S(1)} %add_add_fusion, f32[2,6,256]{2,1,0:T(8,128)S(1)} %maximum_maximum_fusion), kind=kOutput, calls=%fused_computation.32 | convolution fusion | flops 103809024 | bytes 4349952 | tf_op jit(solution)/shard_map/shqk,skhd->sqhd/dot_general | solution.py:39
  82.9 2.7 %copy-done.2 = f32[2,6,256,1024]{3,2,1,0:T(8,128)S(1)} copy-done((f32[2,6,256,1024]{3,2,1,0:T(8,128)S(1)}, f32[2,6,256,1024]{3,2,1,0:T(8,128)}, u32[]{:S(2)}) %copy-start.2) | copy-done | bytes 12582936
  85.6 5.7 %fusion.16 = f32[2,256,6,64]{1,3,2,0:T(8,128)S(1)} fusion(bf16[2,1024,6,64]{3,2,1,0:T(8,128)(2,1)} %reshape_reshape_squeeze.7, f32[2,6,256,1024]{3,2,1,0:T(8,128)S(1)} %copy-done.2, f32[2,6,256]{2,1,0:T(8,128)S(1)} %add_add_fusion, f32[2,6,256]{2,1,0:T(8,128)S(1)} %maximum_maximum_fusion, pred[2,1024]{1,0:T(4,128)(4,1)S(1)} %tile.9), kind=kOutput, calls=%fused_computation.36 | convolution fusion | flops 418381824 | bytes 14968832 | tf_op jit(solution)/shard_map/shqk,skhd->sqhd/dot_general | solution.py:39
  92.0 2.2 %convolution_convert_fusion.1 = bf16[2,256,1536]{2,1,0:T(8,128)(2,1)} fusion(bf16[2,256,384]{1,2,0:T(8,128)(2,1)S(1)} %bitcast.116, bf16[1,384,1536]{2,1,0:T(8,128)(2,1)S(1)} %copy-done), kind=kOutput, calls=%fused_computation.15 | convolution fusion | flops 604766208 | bytes 3145728 | tf_op jit(solution)/shard_map/dot_general | solution.py:121
  94.1 4.9 %copy.105 = bf16[2,256,1536]{1,0,2:T(2,128)(2,1)} copy(bf16[2,256,1536]{2,1,0:T(8,128)(2,1)} %convolution_convert_fusion.1) | data formatting | bytes 3145728
  99.0 2.9 %copy.111 = bf16[192,8,2,256]{3,1,2,0:T(8,128)(2,1)} copy(bf16[192,8,2,256]{3,2,1,0:T(2,128)(2,1)} %bitcast.99) | data formatting | bytes 3145728
  101.9 2.1 %convert_element_type.74 = f32[1,2,256,1536]{3,2,1,0:T(8,128)} convert(bf16[1,2,256,1536]{3,2,1,0:T(8,128)(2,1)S(1)} %copy-done.3) | non-fusion elementwise | flops 786432 | bytes 4718592 | tf_op jit(solution)/shard_map/convert_element_type | solution.py:65
  104.7 33.7 %reduce-scatter.4.cloned.1.call-done = bf16[384,512]{1,0:T(8,128)(2,1)} async-done(((bf16[1536,512]{1,0:T(8,128)(2,1)}), bf16[384,512]{1,0:T(8,128)(2,1)}) %reduce-scatter.4.cloned.1.call-update) | async-done | bytes 393232
  140.2 2.0 %fusion.25 = bf16[2,256,384]{2,1,0:T(8,128)(2,1)} fusion(bf16[2,256,384]{2,1,0:T(8,128)(2,1)S(1)} %copy.106, f32[1,2,256,1536]{3,2,1,0:T(8,128)} %convert_element_type.74, s32[]{:T(128)S(6)} %select_n.56, f32[2,384]{1,0:T(2,128)S(1)} %convert_bitcast_fusion), kind=kLoop, calls=%fused_computation.46 | loop fusion | flops 786432 | bytes 1575940 | tf_op jit(solution)/shard_map/convert_element_type | solution.py:138
  142.2 2.9 %copy.97 = bf16[2,256,2,384]{3,2,0,1:T(2,128)(2,1)} copy(bf16[2,256,2,384]{1,0,3,2:T(2,128)(2,1)S(1)} %slice-done) | data formatting | bytes 1572864 | tf_op jit(solution)/shard_map/stack | solution.py:80
  145.1 3.7 %all-to-all-start.1 = ((bf16[2,256,2,384]{3,2,0,1:T(2,128)(2,1)}), bf16[2,256,2,384]{3,2,0,1:T(2,128)(2,1)S(1)}, u32[]{:S(2)}, u32[]{:S(2)}) async-start(bf16[2,256,2,384]{3,2,0,1:T(2,128)(2,1)} %copy.97), calls=%async_computation.1 | async-start | bytes 1572864 | tf_op jit(solution)/shard_map/all_to_all | solution.py:81
  151.4 5.5 %collective-permute-done.1 = bf16[2,128,384]{2,1,0:T(8,128)(2,1)S(1)} collective-permute-done((bf16[2,128,384]{2,1,0:T(8,128)(2,1)S(1)}, bf16[2,128,384]{2,1,0:T(8,128)(2,1)S(1)}, u32[]{:S(2)}, u32[]{:S(2)}) %collective-permute-start.1) | collective-permute-done | bytes 196640 | tf_op jit(solution)/shard_map/ppermute | solution.py:145
  160.5 1.7 copy.101
  162.3 14.6 %collective-permute-done.2 = bf16[2,128,768]{2,1,0:T(8,128)(2,1)S(1)} collective-permute-done((bf16[2,128,768]{2,1,0:T(8,128)(2,1)S(1)}, bf16[2,128,768]{2,1,0:T(8,128)(2,1)S(1)}, u32[]{:S(2)}, u32[]{:S(2)}) %collective-permute-start.2) | collective-permute-done | bytes 393248 | tf_op jit(solution)/shard_map/ppermute | solution.py:145
  (94 shorter events, 20.0 us)
Async XLA Ops:
  7.2 84.8 %copy-start = (bf16[1,384,1536]{2,1,0:T(8,128)(2,1)S(1)}, bf16[1,384,1536]{2,1,0:T(8,128)(2,1)}, u32[]{:S(2)}) copy-start(bf16[1,384,1536]{2,1,0:T(8,128)(2,1)} %param.16) | copy-start | bytes 3538948
  7.2 5.5 %copy-start.18 = (s32[4,4]{1,0:T(4,128)S(1)}, s32[4,4]{1,0:T(4,128)}, u32[]{:S(2)}) copy-start(s32[4,4]{1,0:T(4,128)} %param.20) | copy-start | bytes 196
  7.2 6.2 %copy-start.17 = (bf16[1,2,2,1536]{3,2,1,0:T(2,128)(2,1)S(1)}, bf16[1,2,2,1536]{3,2,1,0:T(2,128)(2,1)}, u32[]{:S(2)}) copy-start(bf16[1,2,2,1536]{3,2,1,0:T(2,128)(2,1)} %param.13) | copy-start | bytes 36868
  7.2 6.3 %copy-start.3 = (bf16[1,2,256,1536]{3,2,1,0:T(8,128)(2,1)S(1)}, bf16[1,2,256,1536]{3,2,1,0:T(8,128)(2,1)}, u32[]{:S(2)}) copy-start(bf16[1,2,256,1536]{3,2,1,0:T(8,128)(2,1)} %param.12) | copy-start | bytes 4718596
  7.2 42.6 %all-to-all-start = ((bf16[8,64,4,2,384]{4,3,2,1,0:T(2,128)(2,1)}), bf16[8,64,4,2,384]{4,3,2,1,0:T(2,128)(2,1)}, u32[]{:S(2)}, u32[]{:S(2)}) async-start(bf16[8,64,4,2,384]{4,3,2,1,0:T(2,128)(2,1)} %bitcast.105), calls=%async_computation | async-start | bytes 6291456 | tf_op jit(solution)/shard_map/all_to_all | solution.py:84
  12.6 125.8 %reduce-scatter.4.cloned.1.call-start = ((), (), s32[]{:S(2)}) async-start(), calls=%async_computation.3 | async-start | bytes 1966080
  32.4 2.9 %copy-start.7 = (bf16[1,2,154,2,384]{4,3,2,1,0:T(2,128)(2,1)S(1)}, bf16[1,2,154,2,384]{4,3,2,1,0:T(2,128)(2,1)}, u32[]{:S(2)}) copy-start(bf16[1,2,154,2,384]{4,3,2,1,0:T(2,128)(2,1)} %param.18) | copy-start | bytes 1419268
  35.3 6.4 %copy-start.19 = (s32[2]{0:T(128)S(1)}, s32[2]{0:T(128)}, u32[]{:S(2)}) copy-start(s32[2]{0:T(128)} %param.19) | copy-start | bytes 28
  39.7 5.6 %copy-start.8 = (bf16[2,256,1,384]{1,3,0,2:T(8,128)(2,1)S(1)}, bf16[2,256,1,384]{1,3,0,2:T(8,128)(2,1)}, u32[]{:S(2)}) copy-start(bf16[2,256,1,384]{1,3,0,2:T(8,128)(2,1)} %copy.89) | copy-start | bytes 1179652
  62.1 4.5 %copy-start.12 = (f32[2,6,256]{2,1,0:T(8,128)S(1)}, f32[2,6,256]{2,1,0:T(8,128)}, u32[]{:S(2)}) copy-start(f32[2,6,256]{2,1,0:T(8,128)} %get-tuple-element.27) | copy-start | bytes 36868
  62.1 4.5 %copy-start.13 = (f32[2,6,256]{2,1,0:T(8,128)S(1)}, f32[2,6,256]{2,1,0:T(8,128)}, u32[]{:S(2)}) copy-start(f32[2,6,256]{2,1,0:T(8,128)} %get-tuple-element.29) | copy-start | bytes 36868
  66.5 5.3 %copy-start.1 = (f32[2,6,256,1024]{3,2,1,0:T(8,128)}, f32[2,6,256,1024]{3,2,1,0:T(8,128)S(1)}, u32[]{:S(2)}) copy-start(f32[2,6,256,1024]{3,2,1,0:T(8,128)S(1)} %get-tuple-element.26) | copy-start | bytes 37748740
  66.5 5.3 %copy-start.4 = (f32[2,6,256,256]{2,3,1,0:T(8,128)S(1)}, f32[2,6,256,256]{2,3,1,0:T(8,128)}, u32[]{:S(2)}) copy-start(f32[2,6,256,256]{2,3,1,0:T(8,128)} %get-tuple-element.30) | copy-start | bytes 9437188
  71.8 1.5 copy-start.5
  73.9 6.2 %copy-start.10 = (bf16[2,256,1,384]{1,3,0,2:T(8,128)(2,1)S(1)}, bf16[2,256,1,384]{1,3,0,2:T(8,128)(2,1)}, u32[]{:S(2)}) copy-start(bf16[2,256,1,384]{1,3,0,2:T(8,128)(2,1)} %copy.93) | copy-start | bytes 1179652
  80.0 5.5 %copy-start.2 = (f32[2,6,256,1024]{3,2,1,0:T(8,128)S(1)}, f32[2,6,256,1024]{3,2,1,0:T(8,128)}, u32[]{:S(2)}) copy-start(f32[2,6,256,1024]{3,2,1,0:T(8,128)} %copy-done.1) | copy-start | bytes 37748740
  85.6 5.7 %copy-start.6 = (f32[2,6,256,154]{2,3,1,0:T(8,128)S(1)}, f32[2,6,256,154]{2,3,1,0:T(8,128)}, u32[]{:S(2)}) copy-start(f32[2,6,256,154]{2,3,1,0:T(8,128)} %get-tuple-element.28) | copy-start | bytes 5677060
  85.6 5.7 %copy-start.9 = (bf16[2,154,1,384]{1,3,0,2:T(8,128)(2,1)S(1)}, bf16[2,154,1,384]{1,3,0,2:T(8,128)(2,1)}, u32[]{:S(2)}) copy-start(bf16[2,154,1,384]{1,3,0,2:T(8,128)(2,1)} %copy.92) | copy-start | bytes 709636
  104.7 37.5 %slice-start = ((bf16[2,256,3,384]{1,0,3,2:T(2,128)(2,1)}), bf16[2,256,2,384]{1,0,3,2:T(2,128)(2,1)S(1)}, s32[]{:S(2)}) async-start(bf16[2,256,3,384]{1,0,3,2:T(2,128)(2,1)} %reshape.258), calls=%async_computation.4 | async-start | bytes 1572864 | tf_op jit(solution)/shard_map/stack | solution.py:80
  142.2 6.6 %copy-start.15 = (bf16[2,2,1536]{2,1,0:T(2,128)(2,1)S(1)}, bf16[2,2,1536]{2,1,0:T(2,128)(2,1)}, u32[]{:S(2)}) copy-start(bf16[2,2,1536]{2,1,0:T(2,128)(2,1)} %param.21) | copy-start | bytes 36868
  142.2 6.6 %collective-permute-start = (bf16[2,256,384]{2,1,0:T(8,128)(2,1)}, bf16[2,256,384]{2,1,0:T(8,128)(2,1)S(1)}, u32[]{:S(2)}, u32[]{:S(2)}) collective-permute-start(bf16[2,256,384]{2,1,0:T(8,128)(2,1)} %fusion.25), channel_id=1, source_target_pairs={{0,16},{16,0},{1,17},{17,1},{2,18},{18,2},{3,19},{19,3},{4,20},{20... | collective-permute-start | bytes 1179656 | tf_op jit(solution)/shard_map/ppermute | solution.py:14
  145.1 15.2 %all-to-all-start.1 = ((bf16[2,256,2,384]{3,2,0,1:T(2,128)(2,1)}), bf16[2,256,2,384]{3,2,0,1:T(2,128)(2,1)S(1)}, u32[]{:S(2)}, u32[]{:S(2)}) async-start(bf16[2,256,2,384]{3,2,0,1:T(2,128)(2,1)} %copy.97), calls=%async_computation.1 | async-start | bytes 1572864 | tf_op jit(solution)/shard_map/all_to_all | solution.py:81
  149.8 7.2 %collective-permute-start.1 = (bf16[2,128,384]{2,1,0:T(8,128)(2,1)S(1)}, bf16[2,128,384]{2,1,0:T(8,128)(2,1)S(1)}, u32[]{:S(2)}, u32[]{:S(2)}) collective-permute-start(bf16[2,128,384]{2,1,0:T(8,128)(2,1)S(1)} %dynamic-slice_select_fusion), channel_id=1, source_target_pairs={{0,4},{4,0},{8,12},{12,8},{1,5},{5,1},{9,13},{13,9},{2,6},{6,2},{1... | collective-permute-start | bytes 589832 | tf_op jit(solution)/shard_map/ppermute | solution.py:145
  157.1 19.8 %collective-permute-start.2 = (bf16[2,128,768]{2,1,0:T(8,128)(2,1)S(1)}, bf16[2,128,768]{2,1,0:T(8,128)(2,1)S(1)}, u32[]{:S(2)}, u32[]{:S(2)}) collective-permute-start(bf16[2,128,768]{2,1,0:T(8,128)(2,1)S(1)} %maximum_select_fusion.3), channel_id=1, source_target_pairs={{0,8},{4,12},{8,0},{12,4},{1,9},{5,13},{9,1},{13,5},{2,10},{6,14},... | collective-permute-start | bytes 1179656 | tf_op jit(solution)/shard_map/ppermute | solution.py:145
  160.5 17.0 %copy-start.14 = (f32[2,1536]{1,0:T(2,128)S(1)}, f32[2,1536]{1,0:T(2,128)}, u32[]{:S(2)}) copy-start(f32[2,1536]{1,0:T(2,128)} %get-tuple-element.34) | copy-start | bytes 36868
  162.2 15.7 %copy-start.11 = (bf16[1536,64]{0,1:T(8,128)(2,1)S(1)}, bf16[1536,64]{0,1:T(8,128)(2,1)}, u32[]{:S(2)}) copy-start(bf16[1536,64]{0,1:T(8,128)(2,1)} %param.22) | copy-start | bytes 589828
  162.3 16.1 %copy-start.16 = (f32[1,64,128]{2,1,0:T(8,128)S(1)}, f32[1,64,128]{2,1,0:T(8,128)}, u32[]{:S(2)}) copy-start(f32[1,64,128]{2,1,0:T(8,128)} %param.23) | copy-start | bytes 98308
Sparse Core Ops, SparseCore 0:
  102.0 36.3 reduce-scatter.3
